TPU v7x, 32 devices: a whole 2x2x4 slice. The times are simulated.
32 devices in a mesh: group: 2 (over y), seq: 8 (over z, x), tp: 2 (over core).
Axes of the slice: x: 2, y: 2, z: 4, core: 2. Of those that a mesh axis runs over, the one named last changes fastest.
Arguments:
- hidden: bfloat16 [4096, 7168], P(('group', 'seq', 'tp')), parts along dimension 0, may hold values from -6 to 6
- in_gain: bfloat16 [7168], replicated, may hold values from 0.099609375 to 1.8984375
- kv_weight: bfloat16 [7168, 576], P('seq', 'tp'), may hold values from -0.0625 to 0.0625
- kv_gain: bfloat16 [512], replicated, may hold values from 0.099609375 to 1.8984375
- block_owner: int32 [32], replicated, may hold values from 0 to 7, as said below
- block_slot: int32 [32], replicated, may hold values from 0 to 7, as said below
Outputs:
- owner_cache: bfloat16 [128, 64, 576], P(('group', 'seq'), None, 'tp'), parts along dimension 0
- owner_scales: bfloat16 [128, 64], P(('group', 'seq')), parts along dimension 0
There are 2 independent parts, one for each index of `group`. A program takes and returns all parts, laid end to end along the dimension named above; an argument that names none is the same for every part. Nothing has to cross between parts.
Inputs may be any that keep to these rules, and one draw needn't show every extreme that they name: `block_owner`: each owner is named by 0 or 2 of the 4 blocks of one index of seq, so at most 2 from one device; every owner receives at most 8 blocks, and some owner exactly that many; loads are uneven. `block_slot`: the slots named for one owner are distinct.
All inputs are finite; a program needn't handle non-finite values. Where the computation divides by a largest or mean magnitude, that divisor is 1e-20 or more.
Results may differ from a plain program's by a relative error of at most 0.0085.
Values may be sent and summed in bfloat16 or wider, within the bound.
A program may use at most 128 MiB of HBM per device.

v0:
```python
import math

import jax
import jax.numpy as jnp
import numpy as np
from jax import lax
from jax.sharding import PartitionSpec as P

LAT = 512
ROPE = 64
SEND_CAP = 2


EPSILON = 1e-06


def rope_periods(rope_width):
    return np.floor(
        2.0 * np.pi * 10000.0 ** (np.arange(rope_width // 2) * 2.0 / rope_width) + 0.5
    ).astype(np.int32)


def normalize(values, in_gain):
    wide = values.astype(jnp.float32)
    power = jnp.mean(wide * wide, axis=1, keepdims=True)
    return (wide * lax.rsqrt(power + EPSILON) * in_gain.astype(jnp.float32)).astype(jnp.bfloat16)


def shape_latent(projected, power, gain_cols, positions, col_index):
    scaled = projected * lax.rsqrt(power / LAT + EPSILON)[:, None] * gain_cols[None, :]
    periods = jnp.asarray(rope_periods(ROPE))
    phase = (
        (positions[:, None] % periods[None, :]).astype(jnp.float32)
        * (2.0 * math.pi)
        / periods.astype(jnp.float32)
    )
    cosine = jnp.cos(phase)
    sine = jnp.sin(phase)
    col_total = projected.shape[1]
    rope_tail = projected[:, col_total - ROPE :]
    lower_half = rope_tail[:, : ROPE // 2]
    upper_half = rope_tail[:, ROPE // 2 :]
    rotated = jnp.concatenate(
        [lower_half * cosine - upper_half * sine, upper_half * cosine + lower_half * sine], axis=1
    )
    rotated_full = jnp.concatenate([projected[:, : col_total - ROPE], rotated], axis=1)
    return jnp.where((col_index >= LAT)[None, :], rotated_full, scaled)


def hand_off(quant, token_scale, block_owner, block_slot):
    seq_count = lax.axis_size("seq")
    seq_index = lax.axis_index("seq")
    block_count = quant.shape[0] // 64
    col_width = quant.shape[1]
    blocks_flat = quant.reshape(block_count, 64 * col_width)
    scales_flat = token_scale.reshape(block_count, 64)
    owner_grid = block_owner.reshape(seq_count, block_count)
    slot_grid = block_slot.reshape(seq_count, block_count)
    earlier = (jnp.arange(block_count)[:, None] < jnp.arange(block_count)[None, :]).astype(
        jnp.int32
    )
    own_row = lax.dynamic_slice_in_dim(owner_grid, seq_index, 1, 0)[0]
    same_owner = (own_row[:, None] == own_row[None, :]).astype(jnp.int32)
    send_rank = jnp.sum(same_owner * earlier, axis=0)
    targets = jnp.arange(seq_count, dtype=jnp.int32)
    ranks = jnp.arange(SEND_CAP, dtype=jnp.int32)
    select = (own_row[None, None, :] == targets[:, None, None]) & (
        send_rank[None, None, :] == ranks[None, :, None]
    )
    select = select.reshape(seq_count * SEND_CAP, block_count).astype(jnp.bfloat16)
    outgoing = jnp.dot(select, blocks_flat, preferred_element_type=jnp.float32).astype(jnp.bfloat16)
    outgoing_scales = jnp.dot(select, scales_flat, preferred_element_type=jnp.float32).astype(
        jnp.bfloat16
    )
    outgoing = outgoing.reshape(seq_count, SEND_CAP * 64 * col_width)
    outgoing_scales = outgoing_scales.reshape(seq_count, SEND_CAP * 64)
    incoming, incoming_scales = (
        lax.all_to_all(outgoing, "seq", split_axis=0, concat_axis=0, tiled=True),
        lax.all_to_all(outgoing_scales, "seq", split_axis=0, concat_axis=0, tiled=True),
    )
    owned_flags = (owner_grid == seq_index).astype(jnp.int32)
    recv_rank = jnp.sum(owned_flags[:, :, None] * earlier[None, :, :], axis=1)
    slot_hits = (owned_flags[:, None, :] == 1) & (recv_rank[:, None, :] == ranks[None, :, None])
    slot_of = jnp.sum(jnp.where(slot_hits, slot_grid[:, None, :] + 1, 0), axis=2) - 1
    slot_total = 2 * block_count
    placing = (
        slot_of.reshape(-1)[None, :] == jnp.arange(slot_total, dtype=jnp.int32)[:, None]
    ).astype(jnp.bfloat16)
    owner_cache = jnp.dot(
        placing,
        incoming.reshape(seq_count * SEND_CAP, 64 * col_width),
        preferred_element_type=jnp.float32,
    )
    owner_cache = owner_cache.astype(jnp.bfloat16).reshape(slot_total, 64, col_width)
    owner_scales = jnp.dot(
        placing,
        incoming_scales.reshape(seq_count * SEND_CAP, 64),
        preferred_element_type=jnp.float32,
    )
    return (owner_cache, owner_scales.astype(jnp.bfloat16))


def per_device(hidden, in_gain, kv_weight, kv_gain, block_owner, block_slot):
    seq_index = lax.axis_index("seq")
    tp_index = lax.axis_index("tp")
    gain_full = jnp.concatenate([kv_gain.astype(jnp.float32), jnp.ones((ROPE,), jnp.float32)])
    shard_rows = lax.all_gather(hidden, "tp", axis=0, tiled=True)
    normed = normalize(shard_rows, in_gain)
    row_total = shard_rows.shape[0]
    col_half = kv_weight.shape[1]
    projected = jnp.dot(
        normed,
        lax.all_gather(kv_weight, "seq", axis=0, tiled=True),
        preferred_element_type=jnp.float32,
    )
    col_index = tp_index * col_half + jnp.arange(col_half, dtype=jnp.int32)
    latent_part = jnp.where((col_index < LAT)[None, :], projected * projected, 0.0)
    power = lax.psum(jnp.sum(latent_part, axis=1), "tp")
    gain_cols = lax.dynamic_slice_in_dim(gain_full, tp_index * col_half, col_half, 0)
    positions = seq_index * row_total + jnp.arange(row_total, dtype=jnp.int32)
    shaped = shape_latent(projected, power, gain_cols, positions, col_index)
    token_peak = lax.pmax(jnp.max(jnp.abs(shaped), axis=1), "tp")
    token_scale = (token_peak + EPSILON).astype(jnp.bfloat16)
    quant = (shaped / token_scale.astype(jnp.float32)[:, None]).astype(jnp.bfloat16)
    return hand_off(quant, token_scale, block_owner, block_slot)


def solution(mesh):
    return jax.shard_map(
        per_device,
        mesh=mesh,
        in_specs=(P(("group", "seq", "tp"), None), P(), P("seq", "tp"), P(), P(), P()),
        out_specs=(P(("group", "seq"), None, "tp"), P(("group", "seq"), None)),
        check_vma=False,
    )
```

profile of v0, /device:TPU:0, one launch (start us, length us, event | category | flops | bytes accessed | tf_op | source)
XLA Modules:
  0.0 158.5 jit_solution(144533938531431405)
XLA Ops:
  7.2 0.7 all-gather.3.cloned.1.call-update
  7.9 0.7 all-gather.5.cloned.1.call-update
  8.7 0.7 convert_element_type.64
  9.4 0.7 reshape.169
  10.5 0.7 pad_convert_fusion
  11.3 13.9 %all-gather.3.cloned.1.call-done = bf16[256,7168]{1,0:T(8,128)(2,1)} async-done(((bf16[128,7168]{1,0:T(8,128)(2,1)}), bf16[256,7168]{1,0:T(8,128)(2,1)}) %all-gather.3.cloned.1.call-update) | async-done | bytes 3670032 | tf_op jit(solution)/shard_map/all_gather | solution.py:107
  25.2 2.8 %fusion = f32[256]{0:T(256)S(1)} fusion(bf16[256,7168]{1,0:T(8,128)(2,1)} %all-gather.3.cloned.1.call-done), kind=kLoop, calls=%fused_computation.4 | loop fusion | flops 5504768 | bytes 3671040 | tf_op jit(solution)/shard_map/reduce_sum | solution.py:25
  28.1 72.8 %all-gather.5.cloned.1.call-done = bf16[7168,288]{0,1:T(8,128)(2,1)} async-done(((bf16[896,288]{0,1:T(8,128)(2,1)}), bf16[7168,288]{0,1:T(8,128)(2,1)}) %all-gather.5.cloned.1.call-update) | async-done | bytes 4128784 | tf_op jit(solution)/shard_map/all_gather | solution.py:113
  100.9 4.7 %select_reduce_fusion = (f32[256]{0:T(256)S(1)}, f32[256,288]{0,1:T(8,128)S(1)}) fusion(pred[288]{0:T(512)(128)(4,1)S(1)} %fusion.14, bf16[7168,288]{0,1:T(8,128)(2,1)} %all-gather.5.cloned.1.call-done, bf16[256,7168]{1,0:T(8,128)(2,1)} %all-gather.3.cloned.1.call-done, f32[7168]{0:T(1024)S(1)} %convert_element_type.64, f32[256]{0:T(256)S(1)} %add_rsqrt_fusion.1), kind=kOutput, calls=%fused_computation.15 | convolution fusion | flops 1064525568 | bytes 8124704 | tf_op jit(solution)/shard_map/dot_general | solution.py:111
  105.6 2.5 %psum.7 = f32[256]{0:T(256)S(1)} all-reduce(f32[256]{0:T(256)S(1)} %get-tuple-element.10), channel_id=1, replica_groups=mesh['group'=2,'seq'=8,'tp'=2] {'tp'}, use_global_device_ids=true, to_apply=%region_5.6 | all-reduce | flops 256 | bytes 2048 | tf_op jit(solution)/shard_map/psum | solution.py:118
  108.0 0.6 multiply_subtract_fusion
  108.6 0.2 abs_reduce_fusion
  108.8 2.5 %pmax.7 = f32[256]{0:T(256)S(1)} all-reduce(f32[256]{0:T(256)S(1)} %get-tuple-element.6), channel_id=1, replica_groups=mesh['group'=2,'seq'=8,'tp'=2] {'tp'}, use_global_device_ids=true, to_apply=%region_7.8 | all-reduce | flops 256 | bytes 2048 | tf_op jit(solution)/shard_map/pmax | solution.py:122
  111.3 0.2 copy.20
  111.5 0.3 reshape.170
  111.9 0.2 convolution_convert_fusion.2
  112.1 0.7 all_to_all.17
  112.7 3.3 %all-to-all-start.1 = ((bf16[8,1,128]{2,1,0:T(2,128)(2,1)}), bf16[8,1,128]{2,1,0:T(2,128)(2,1)S(1)}, u32[]{:S(2)}, u32[]{:S(2)}) async-start(bf16[8,1,128]{2,1,0:T(2,128)(2,1)} %all_to_all.17), calls=%async_computation.1 | async-start | bytes 8192 | tf_op jit(solution)/shard_map/all_to_all | solution.py:79
  116.1 0.4 convolution_convert_fusion
  116.5 0.9 all_to_all.16
  117.4 0.5 broadcast.148
  117.9 4.4 %reduce.2 = bf16[8,36864]{1,0:T(8,128)(2,1)S(1)} reduce(bf16[8,1,36864]{2,1,0:T(2,128)(2,1)S(1)} %all_to_all.16, bf16[]{:T(256)} %broadcast.148), dimensions={1}, to_apply=%all_to_all.16.reduce_sub_computation | reduce | bytes 1179650 | tf_op jit(solution)/shard_map/all_to_all | solution.py:78
  122.3 1.2 reshape.177
  123.6 5.9 %all-to-all-start = ((bf16[8,2,18432]{2,1,0:T(2,128)(2,1)}), bf16[8,2,18432]{2,1,0:T(2,128)(2,1)S(1)}, u32[]{:S(2)}, u32[]{:S(2)}) async-start(bf16[8,2,18432]{2,1,0:T(2,128)(2,1)} %reshape.177), calls=%async_computation | async-start | bytes 1179648 | tf_op jit(solution)/shard_map/all_to_all | solution.py:78
  129.6 0.1 copy.16
  130.2 0.7 convolution_convert_fusion.3
  131.0 14.5 %all-to-all-done = bf16[8,2,18432]{2,1,0:T(2,128)(2,1)S(1)} async-done(((bf16[8,2,18432]{2,1,0:T(2,128)(2,1)}), bf16[8,2,18432]{2,1,0:T(2,128)(2,1)S(1)}, u32[]{:S(2)}, u32[]{:S(2)}) %all-to-all-start) | async-done | bytes 589856 | tf_op jit(solution)/shard_map/all_to_all | solution.py:78
  145.4 0.6 reshape.178
  146.0 3.7 %reduce = bf16[8,36864]{1,0:T(8,128)(2,1)S(1)} reduce(bf16[8,1,36864]{2,1,0:T(2,128)(2,1)S(1)} %reshape.178, bf16[]{:T(256)} %constant.61), dimensions={1}, to_apply=%all_to_all.13.reduce_sub_computation | reduce | bytes 1179650 | tf_op jit(solution)/shard_map/all_to_all | solution.py:78
  149.8 0.2 reshape.171
  150.0 0.2 convolution_convert_fusion.1
  150.2 1.4 reshape.172
  (38 shorter events, 1.4 us)
Async XLA Ops:
  7.2 18.0 %all-gather.3.cloned.1.call-start = ((), (), s32[]{:S(2)}) async-start(), calls=%async_computation.2 | async-start | bytes 5505024 | tf_op jit(solution)/shard_map/all_gather | solution.py:107
  7.9 93.0 %all-gather.5.cloned.1.call-start = ((), (), s32[]{:S(2)}) async-start(), calls=%async_computation.3 | async-start | bytes 4644864 | tf_op jit(solution)/shard_map/all_gather | solution.py:113
  28.0 80.0 %copy-start = (s32[32]{0:T(128)S(1)}, s32[32]{0:T(128)}, u32[]{:S(2)}) copy-start(s32[32]{0:T(128)} %constant.56) | copy-start | bytes 388
  28.0 80.0 %copy-start.1 = (f32[32]{0:T(128)S(1)}, f32[32]{0:T(128)}, u32[]{:S(2)}) copy-start(f32[32]{0:T(128)} %constant.60) | copy-start | bytes 388
  108.8 20.9 %copy-start.2 = (s32[32]{0:T(128)S(1)}, s32[32]{0:T(128)}, u32[]{:S(2)}) copy-start(s32[32]{0:T(128)} %param.12) | copy-start | bytes 388
  112.7 10.8 %all-to-all-start.1 = ((bf16[8,1,128]{2,1,0:T(2,128)(2,1)}), bf16[8,1,128]{2,1,0:T(2,128)(2,1)S(1)}, u32[]{:S(2)}, u32[]{:S(2)}) async-start(bf16[8,1,128]{2,1,0:T(2,128)(2,1)} %all_to_all.17), calls=%async_computation.1 | async-start | bytes 8192 | tf_op jit(solution)/shard_map/all_to_all | solution.py:79
  123.6 21.9 %all-to-all-start = ((bf16[8,2,18432]{2,1,0:T(2,128)(2,1)}), bf16[8,2,18432]{2,1,0:T(2,128)(2,1)S(1)}, u32[]{:S(2)}, u32[]{:S(2)}) async-start(bf16[8,2,18432]{2,1,0:T(2,128)(2,1)} %reshape.177), calls=%async_computation | async-start | bytes 1179648 | tf_op jit(solution)/shard_map/all_to_all | solution.py:78
Sparse Core Ops, SparseCore 0:
  9.5 15.5 all-gather.2
  27.3 73.4 all-gather.4
where the time goes:
time: 159 us; the launch traced here: 158 us
  waiting for transfers between devices  103 us (65%)
  between operations  14.2 us (9%)
  other arithmetic  13.6 us (9%)
  starting transfers between devices  9.32 us (6%)
  local copies, waits for them, and re-layouts  7.64 us (5%)
  matrix products  6.19 us (4%)
  blocking collectives  4.94 us (3%)
    all_gather x1, waiting for transfers between devices, per_device(): lax.all_gather(kv_weight, 'seq', axis=0, tiled=True)  72.8 us
    all_to_all x1, waiting for transfers between devices, hand_off(): lax.all_to_all(outgoing, 'seq', split_axis=0, concat_axis=0, tiled=True)  14.5 us
    all_gather x1, waiting for transfers between devices, per_device(): shard_rows = lax.all_gather(hidden, 'tp', axis=0, tiled=True)  13.9 us
    all_to_all x2, other arithmetic, hand_off(): lax.all_to_all(outgoing, 'seq', split_axis=0, concat_axis=0, tiled=True)  8.12 us
    all_to_all x1, starting transfers between devices, hand_off(): lax.all_to_all(outgoing, 'seq', split_axis=0, concat_axis=0, tiled=True)  5.93 us
    dot_general x1, matrix products, per_device(): jnp.dot(normed, lax.all_gather(kv_weight, 'seq', axis=0, tiled=True), pre...  4.67 us
    all_to_all x1, starting transfers between devices, hand_off(): lax.all_to_all(outgoing_scales, 'seq', split_axis=0, concat_axis=0, tiled...  3.31 us
  transfers between devices with their start and end apart: 4, of which 3 were waited for; matrix products, arithmetic and copies ran while one was open for 9% of the time, Pallas kernels for 0%

commit v1 on v0

--- a/solution.py
+++ b/solution.py
@@ -1,9 +1,12 @@
+import functools
 import math
 
 import jax
 import jax.numpy as jnp
 import numpy as np
 from jax import lax
+from jax.experimental import pallas as pl
+from jax.experimental.pallas import tpu as pltpu
 from jax.sharding import PartitionSpec as P
 
 LAT = 512
@@ -125,9 +128,330 @@
     return hand_off(quant, token_scale, block_owner, block_slot)
 
 
+MESH = pl.DeviceIdType.MESH
+X_COUNT = 2
+Z_COUNT = 4
+NT = (((1,), (1,)), ((), ()))
+SCALE_ROWS = 16
+
+
+def fused_kernel(
+    owner_ref, slot_ref, hidden_ref, gain_ref, weight_ref, kv_gain_ref,
+    cache_ref, scales_ref,
+    weights, normed, select, placing, outgoing, incoming, stats_out, stats_in,
+    hop_send, weight_recv, normed_sem, stats_sem, block_send, block_recv,
+):
+    group, seq, tp = lax.axis_index("group"), lax.axis_index("seq"), lax.axis_index("tp")
+    n_seq = weights.shape[0]
+    cols, depth = weights.shape[1:]
+    rows = hidden_ref.shape[0]
+    tokens = 2 * rows
+    block_count = tokens // 64
+    chunk = cols // 3
+    z, x = seq // X_COUNT, seq % X_COUNT
+    mine, middle, other = 2 * group, 1, 2 - 2 * group
+
+    def at(z_to, x_to):
+        return (group, z_to * X_COUNT + x_to, tp)
+
+    above, below, beside = at(z + 1, x), at(z - 1, x), at(z, 1 - x)
+    across, twin = (1 - group, seq, tp), (group, seq, 1 - tp)
+
+    barrier = pltpu.get_barrier_semaphore()
+    for step in range(1, n_seq):
+        pl.semaphore_signal(
+            barrier, inc=1, device_id=(group, (seq + step) % n_seq, tp), device_id_type=MESH
+        )
+    for peer in (across, twin):
+        pl.semaphore_signal(barrier, inc=1, device_id=peer, device_id_type=MESH)
+
+    row_id = lax.broadcasted_iota(jnp.int32, (cols, cols), 0)
+    col_id = lax.broadcasted_iota(jnp.int32, (cols, cols), 1)
+    eye = jnp.where(row_id == col_id, 1.0, 0.0).astype(jnp.bfloat16)
+    weights[seq] = lax.dot_general(
+        eye, weight_ref[...], NT, preferred_element_type=jnp.float32
+    ).astype(jnp.bfloat16)
+    pl.semaphore_wait(barrier, n_seq + 1)
+
+    def piece(shard, part, direction, peer):
+        where = weights.at[shard, pl.ds(pl.multiple_of(part * chunk, chunk), chunk), :]
+        return pltpu.make_async_remote_copy(
+            src_ref=where,
+            dst_ref=where,
+            send_sem=hop_send.at[shard, part, direction],
+            recv_sem=weight_recv.at[shard, part],
+            device_id=peer,
+            device_id_type=MESH,
+        )
+
+    def when_inside(z_at, do):
+        pl.when((z_at >= 0) & (z_at < Z_COUNT))(do)
+
+    own = seq
+    for part in (mine, middle):
+        when_inside(z + 1, lambda: piece(own, part, 0, above).start())
+        when_inside(z - 1, lambda: piece(own, part, 1, below).start())
+        piece(own, part, 2, beside).start()
+
+    first = pl.multiple_of(tp * rows, rows)
+
+    def norm_tile(index, carry):
+        tile = hidden_ref[pl.ds(pl.multiple_of(index * 16, 16), 16), :].astype(jnp.float32)
+        power = jnp.mean(tile * tile, axis=1, keepdims=True)
+        out = tile * lax.rsqrt(power + EPSILON) * gain_ref[...].astype(jnp.float32)
+        normed[pl.ds(pl.multiple_of(first + index * 16, 16), 16), :] = out.astype(jnp.bfloat16)
+        return carry
+
+    lax.fori_loop(0, rows // 16, norm_tile, 0)
+    half = normed.at[pl.ds(first, rows), :]
+    normed_copy = pltpu.make_async_remote_copy(
+        src_ref=half, dst_ref=half, send_sem=normed_sem.at[0], recv_sem=normed_sem.at[1],
+        device_id=twin, device_id_type=MESH,
+    )
+    normed_copy.start()
+
+    def rank_of(base, block):
+        same = [
+            jnp.where(owner_ref[base + earlier] == owner_ref[base + block], 1, 0)
+            for earlier in range(block)
+        ]
+        return sum(same, jnp.int32(0))
+
+    lane_id = lax.broadcasted_iota(jnp.int32, (64, n_seq * 128), 1)
+    line_id = lax.broadcasted_iota(jnp.int32, (64, n_seq * 128), 0)
+    for block in range(block_count):
+        place = owner_ref[seq * block_count + block] * 128 + rank_of(seq * block_count, block) * 64
+        select[pl.ds(block * 64, 64), :] = jnp.where(lane_id - line_id == place, 1.0, 0.0).astype(
+            jnp.bfloat16
+        )
+
+    slot_total = cache_ref.shape[0] // 64
+    lane_in = lax.broadcasted_iota(jnp.int32, (slot_total * 64, 128), 1)
+    line_in = lax.broadcasted_iota(jnp.int32, (slot_total * 64, 128), 0)
+
+    def slots_from(source):
+        found = [jnp.int32(-1), jnp.int32(-1)]
+        for block in range(block_count):
+            entry = source * block_count + block
+            rank = rank_of(source * block_count, block)
+            for place in range(SEND_CAP):
+                hit = (owner_ref[entry] == seq) & (rank == place)
+                found[place] = jnp.where(hit, slot_ref[entry], found[place])
+        return found
+
+    slots = [slots_from(source) for source in range(n_seq)]
+    for source in range(n_seq):
+        low, high = slots[source]
+        target = jnp.where(lane_in < 64, low * 64, high * 64) + lane_in % 64
+        placing[:, source * 128 : (source + 1) * 128] = jnp.where(
+            line_in == target, 1.0, 0.0
+        ).astype(jnp.bfloat16)
+
+    rope_half = ROPE // 2
+    positions = lax.broadcasted_iota(jnp.int32, (rope_half, tokens), 1) + seq * tokens
+    positions = positions.astype(jnp.float32)
+    pair = lax.broadcasted_iota(jnp.int32, (rope_half, 1), 0)
+    periods = jnp.zeros((rope_half, 1), jnp.float32)
+    for index, period in enumerate(rope_periods(ROPE)):
+        periods = jnp.where(pair == index, float(period), periods)
+    turns = jnp.floor((positions + 0.5) / periods)
+    phase = (positions - turns * periods) * (2.0 * math.pi) / periods
+    cosine, sine = jnp.cos(phase), jnp.sin(phase)
+
+    column = lax.broadcasted_iota(jnp.int32, (cols, LAT), 0) + tp * cols
+    gain_lane = lax.broadcasted_iota(jnp.int32, (cols, LAT), 1)
+    gain_col = jnp.sum(
+        jnp.where(column == gain_lane, kv_gain_ref[...].astype(jnp.float32), 0.0),
+        axis=1, keepdims=True,
+    )
+
+    def relay(z_from, x_from, onward):
+        def do():
+            shard = z_from * X_COUNT + x_from
+            for part in (mine, middle):
+                piece(shard, part, 2, beside).wait_recv()
+                onward(shard, part)
+                if part is mine:
+                    piece(shard, part, 3, across).start()
+        when_inside(z_from, do)
+
+    def upward(shard, part):
+        when_inside(z + 1, lambda: piece(shard, part, 0, above).start())
+        piece(shard, part, 2, beside).start()
+
+    def downward(shard, part):
+        when_inside(z - 1, lambda: piece(shard, part, 1, below).start())
+        piece(shard, part, 2, beside).start()
+
+    def stop(shard, part):
+        pass
+
+    relay(z, 1 - x, stop)
+    for distance in range(1, Z_COUNT):
+        relay(z - distance, x, upward)
+        relay(z + distance, x, downward)
+        relay(z - distance, 1 - x, stop)
+        relay(z + distance, 1 - x, stop)
+
+    normed_copy.wait()
+    total = jnp.zeros((cols, tokens), jnp.float32)
+    for z_at in (z, z + 1 - 2 * (z % 2), (z + 2) % Z_COUNT, Z_COUNT - 1 - z):
+        for x_at in (x, 1 - x):
+            shard = z_at * X_COUNT + x_at
+            if not (z_at is z and x_at is x):
+                piece(shard, other, 3, across).wait_recv()
+            features = pl.ds(pl.multiple_of(shard * depth, 128), depth)
+            total = total + lax.dot_general(
+                weights[shard], normed[:, features], NT, preferred_element_type=jnp.float32
+            )
+
+    latent = (lax.broadcasted_iota(jnp.int32, (cols, 1), 0) + tp * cols) < LAT
+    gained = total * gain_col
+    power = jnp.sum(jnp.where(latent, total * total, 0.0), axis=0, keepdims=True)
+    latent_peak = jnp.max(jnp.where(latent, jnp.abs(gained), 0.0), axis=0, keepdims=True)
+    lower = total[cols - ROPE : cols - rope_half, :]
+    upper = total[cols - rope_half :, :]
+    turned = jnp.concatenate(
+        [lower * cosine - upper * sine, upper * cosine + lower * sine], axis=0
+    )
+    rope_peak = jnp.max(jnp.abs(turned), axis=0, keepdims=True)
+    rope_peak = jnp.where(tp == 1, rope_peak, 0.0)
+    stats_out[0:1, :] = power
+    stats_out[1:2, :] = latent_peak
+    stats_out[2:3, :] = rope_peak
+    stats_out[3:8, :] = jnp.zeros((5, tokens), jnp.float32)
+    stats_copy = pltpu.make_async_remote_copy(
+        src_ref=stats_out, dst_ref=stats_in, send_sem=stats_sem.at[0], recv_sem=stats_sem.at[1],
+        device_id=twin, device_id_type=MESH,
+    )
+    stats_copy.start()
+    stats_copy.wait()
+    inverse = lax.rsqrt((power + stats_in[0:1, :]) / LAT + EPSILON)
+    peak = jnp.maximum(
+        jnp.maximum(latent_peak, stats_in[1:2, :]) * inverse,
+        jnp.maximum(rope_peak, stats_in[2:3, :]),
+    )
+    scale = (peak + EPSILON).astype(jnp.bfloat16)
+    wide_scale = scale.astype(jnp.float32)
+    shaped = jnp.where(
+        latent,
+        gained * inverse,
+        jnp.concatenate([jnp.zeros((cols - ROPE, tokens), jnp.float32), turned], axis=0),
+    )
+    quant = (shaped / wide_scale).astype(jnp.bfloat16)
+    with_scale = jnp.concatenate(
+        [quant, jnp.broadcast_to(wide_scale, (SCALE_ROWS, tokens)).astype(jnp.bfloat16)], axis=0
+    )
+
+    for target in range(n_seq):
+        outgoing[target] = jnp.dot(
+            with_scale, select[:, target * 128 : (target + 1) * 128],
+            preferred_element_type=jnp.float32,
+        ).astype(jnp.bfloat16)
+
+    def block_copy(source, target):
+        return pltpu.make_async_remote_copy(
+            src_ref=outgoing.at[target], dst_ref=incoming.at[source],
+            send_sem=block_send.at[target], recv_sem=block_recv.at[source],
+            device_id=(group, target, tp), device_id_type=MESH,
+        )
+
+    for step in range(1, n_seq):
+        block_copy(seq, (seq + step) % n_seq).start()
+    incoming[seq] = outgoing[seq]
+    for step in range(1, n_seq):
+        source = (seq + step) % n_seq
+        block_copy(source, source).wait_recv()
+    arrived = jnp.concatenate([incoming[source, :cols, :] for source in range(n_seq)], axis=1)
+    cache_ref[...] = lax.dot_general(
+        placing[...], arrived, NT, preferred_element_type=jnp.float32
+    ).astype(jnp.bfloat16)
+    slot_id = lax.broadcasted_iota(jnp.int32, (slot_total, 128), 0)
+    lane = lax.broadcasted_iota(jnp.int32, (slot_total, 128), 1)
+    placed = jnp.zeros((slot_total, 128), jnp.float32)
+    for source in range(n_seq):
+        low, high = slots[source]
+        hit = slot_id == jnp.where(lane < 64, low, high)
+        values = incoming[source, cols : cols + SCALE_ROWS, :].astype(jnp.float32)
+        placed = placed + jnp.where(hit, values[0:slot_total, :], 0.0)
+    scales_ref[...] = (placed[:, :64] + placed[:, 64:]).astype(jnp.bfloat16)
+
+    for step in range(1, n_seq):
+        block_copy(seq, (seq + step) % n_seq).wait_send()
+    for part in (mine, middle):
+        when_inside(z + 1, lambda: piece(own, part, 0, above).wait_send())
+        when_inside(z - 1, lambda: piece(own, part, 1, below).wait_send())
+        piece(own, part, 2, beside).wait_send()
+
+    def sent(z_from, x_from, direction, z_to, peer):
+        def do():
+            shard = z_from * X_COUNT + x_from
+            for part in (mine, middle):
+                if direction is not None:
+                    when_inside(z_to, lambda: piece(shard, part, direction, peer).wait_send())
+                    piece(shard, part, 2, beside).wait_send()
+            piece(shard, mine, 3, across).wait_send()
+        when_inside(z_from, do)
+
+    sent(z, 1 - x, None, None, None)
+    for distance in range(1, Z_COUNT):
+        sent(z - distance, x, 0, z + 1, above)
+        sent(z + distance, x, 1, z - 1, below)
+        sent(z - distance, 1 - x, None, None, None)
+        sent(z + distance, 1 - x, None, None, None)
+
+
+def fused(hidden, in_gain, kv_weight, kv_gain, block_owner, block_slot):
+    rows, width = hidden.shape
+    depth, cols = kv_weight.shape
+    n_seq = lax.axis_size("seq")
+    tokens = 2 * rows
+    slot_total = 2 * (tokens // 64)
+    padded = cols + SCALE_ROWS
+    vmem = pl.BlockSpec(memory_space=pltpu.VMEM)
+    smem = pl.BlockSpec(memory_space=pltpu.SMEM)
+    cache, scales = pl.pallas_call(
+        fused_kernel,
+        out_shape=(
+            jax.ShapeDtypeStruct((slot_total * 64, cols), jnp.bfloat16),
+            jax.ShapeDtypeStruct((slot_total, 64), jnp.bfloat16),
+        ),
+        in_specs=[smem, smem, vmem, vmem, vmem, vmem],
+        out_specs=(vmem, vmem),
+        scratch_shapes=[
+            pltpu.VMEM((n_seq, cols, depth), jnp.bfloat16),
+            pltpu.VMEM((tokens, width), jnp.bfloat16),
+            pltpu.VMEM((tokens, n_seq * 128), jnp.bfloat16),
+            pltpu.VMEM((slot_total * 64, n_seq * 128), jnp.bfloat16),
+            pltpu.VMEM((n_seq, padded, 128), jnp.bfloat16),
+            pltpu.VMEM((n_seq, padded, 128), jnp.bfloat16),
+            pltpu.VMEM((8, tokens), jnp.float32),
+            pltpu.VMEM((8, tokens), jnp.float32),
+            pltpu.SemaphoreType.DMA((n_seq, 3, 4)),
+            pltpu.SemaphoreType.DMA((n_seq, 3)),
+            pltpu.SemaphoreType.DMA((2,)),
+            pltpu.SemaphoreType.DMA((2,)),
+            pltpu.SemaphoreType.DMA((n_seq,)),
+            pltpu.SemaphoreType.DMA((n_seq,)),
+        ],
+        compiler_params=pltpu.CompilerParams(
+            collective_id=0, has_side_effects=True, vmem_limit_bytes=48 * 1024 * 1024
+        ),
+    )(
+        block_owner, block_slot, hidden, in_gain.reshape(1, width), kv_weight,
+        kv_gain.reshape(1, LAT),
+    )
+    return (cache.reshape(slot_total, 64, cols), scales)
+
+
 def solution(mesh):
+    fits = (
+        mesh.shape["seq"] == X_COUNT * Z_COUNT
+        and mesh.shape["group"] == 2
+        and mesh.shape["tp"] == 2
+    )
     return jax.shard_map(
-        per_device,
+        fused if fits else per_device,
         mesh=mesh,
         in_specs=(P(("group", "seq", "tp"), None), P(), P("seq", "tp"), P(), P(), P()),
         out_specs=(P(("group", "seq"), None, "tp"), P(("group", "seq"), None)),

time: 159 us -> 68.3 us (0.43)
  waiting for transfers between devices: 103 us -> 0 us
  Pallas kernels: 0 us -> 59.9 us
  other arithmetic: 13.6 us -> 0 us
  between operations: 14.2 us -> 0.66 us
  starting transfers between devices: 9.32 us -> 0 us
  matrix products: 6.19 us -> 0 us
  blocking collectives: 4.94 us -> 0 us
    all_gather x2 -> x0, waiting for transfers between devices: 86.7 us -> none  [the longest x1 72.8 us: per_device(): lax.all_gather(kv_weight, 'seq', axis=0, tiled=True)]
    pallas_call x0 -> x1, Pallas kernels: none -> 59.9 us  [fused(): pl.pallas_call(fused_kernel, out_shape=(jax.ShapeDtypeStruct((slot_total...]
    all_to_all x2 -> x0, waiting for transfers between devices: 14.5 us -> none  [the longest x1 14.5 us: hand_off(): lax.all_to_all(outgoing, 'seq', split_axis=0, concat_axis=0, tiled=True)]
    all_to_all x2 -> x0, starting transfers between devices: 9.24 us -> none  [the longest x1 5.93 us: hand_off(): lax.all_to_all(outgoing, 'seq', split_axis=0, concat_axis=0, tiled=True)]
    all_to_all x3 -> x0, other arithmetic: 8.15 us -> none  [the longest x2 8.12 us: hand_off(): lax.all_to_all(outgoing, 'seq', split_axis=0, concat_axis=0, tiled=True)]
    dot_general x5 -> x0, matrix products: 6.19 us -> none  [the longest x1 4.67 us: per_device(): jnp.dot(normed, lax.all_gather(kv_weight, 'seq', axis=0, tiled=True), pre...]
    unnamed x8 -> x9, local copies, waits for them, and re-layouts: 1.84 us -> 5.52 us
    reduce_sum x4 -> x0, other arithmetic: 3.04 us -> none  [the longest x1 2.85 us: normalize(): power = jnp.mean(wide * wide, axis=1, keepdims=True)]
  transfers between devices with their start and end apart: 4 -> 0, of which waited for: 3 -> 0; matrix products, arithmetic and copies ran while one was open for 9% -> 0% of each run, Pallas kernels for 0% -> 0%
where the time goes in v1:
time: 68.3 us; the launch traced here: 67.5 us
  Pallas kernels  59.9 us (88%)
  local copies, waits for them, and re-layouts  6.93 us (10%)
    pallas_call x1, Pallas kernels, fused(): pl.pallas_call(fused_kernel, out_shape=(jax.ShapeDtypeStruct((slot_total...  59.9 us
    unnamed x9, local copies, waits for them, and re-layouts  5.52 us

profile of v1, /device:TPU:0, one launch (start us, length us, event | category | flops | bytes accessed | tf_op | source)
XLA Modules:
  0.0 67.5 jit_solution(6558891365745651684)
XLA Ops:
  0.6 0.7 %reshape.14.kv_gain_ref = bf16[1,512]{1,0:T(2,128)(2,1)S(1)} reshape(bf16[512]{0:T(512)(128)(2,1)} %param.9) | data formatting | bytes 2048 | tf_op jit(solution)/shard_map/reshape | solution.py:442
  1.3 0.7 %reshape.13.gain_ref = bf16[1,7168]{1,0:T(2,128)(2,1)S(1)} reshape(bf16[7168]{0:T(1024)(128)(2,1)} %param.7) | data formatting | bytes 28672 | tf_op jit(solution)/shard_map/reshape | solution.py:441
  2.0 1.4 %copy.8.weight_ref = bf16[896,288]{1,0:T(8,128)(2,1)S(1)} copy(bf16[896,288]{0,1:T(8,128)(2,1)} %param.8) | data formatting | bytes 1032192 | tf_op args[2]
  3.4 0.0 copy-start
  3.4 1.5 %copy-done = bf16[128,7168]{1,0:T(8,128)(2,1)S(1)} copy-done((bf16[128,7168]{1,0:T(8,128)(2,1)S(1)}, bf16[128,7168]{1,0:T(8,128)(2,1)}, u32[]{:S(2)}) %copy-start) | copy-done | bytes 1835032
  4.9 0.0 copy-start.1
  4.9 0.7 copy-done.1
  5.6 0.0 copy-start.2
  5.6 0.7 copy-done.2
  6.2 59.9 %shard_map.77 = (bf16[512,288]{1,0:T(8,128)(2,1)S(1)}, bf16[8,64]{1,0:T(8,128)(2,1)S(1)}) custom-call(s32[32]{0:T(128)S(1)} %copy-done.1, s32[32]{0:T(128)S(1)} %copy-done.2, bf16[128,7168]{1,0:T(8,128)(2,1)S(1)} %copy-done, bf16[1,7168]{1,0:T(2,128)(2,1)S(1)} %reshape.13.gain_ref, bf16[896,288]{1,0:T(8,128)(2,1)S(1)} %copy.8.weight_ref, ...), custom_call_target="tpu_custom_call" | custom-call | tf_op jit(solution)/shard_map/pallas_call | solution.py:413
  66.2 0.7 %copy.11 = bf16[8,64,288]{2,1,0:T(8,128)(2,1)} copy(bf16[8,64,288]{2,1,0:T(8,128)(2,1)S(1)} %bitcast.1) | data formatting | bytes 589824
  66.9 0.6 copy.12
Async XLA Ops:
  3.4 1.5 %copy-start = (bf16[128,7168]{1,0:T(8,128)(2,1)S(1)}, bf16[128,7168]{1,0:T(8,128)(2,1)}, u32[]{:S(2)}) copy-start(bf16[128,7168]{1,0:T(8,128)(2,1)} %hidden_ref.1) | copy-start | bytes 5505028
  4.9 0.7 copy-start.1
  5.6 0.7 copy-start.2

commit v2 on v1

--- a/solution.py
+++ b/solution.py
@@ -136,8 +136,9 @@
 
 
 def fused_kernel(
-    owner_ref, slot_ref, hidden_ref, gain_ref, weight_ref, kv_gain_ref,
+    owner_hbm, slot_hbm, hidden_hbm, gain_hbm, weight_hbm, kv_gain_hbm,
     cache_ref, scales_ref,
+    owner_ref, slot_ref, hidden_ref, gain_ref, kv_gain_ref, gain_row, load_sem,
     weights, normed, select, placing, outgoing, incoming, stats_out, stats_in,
     hop_send, weight_recv, normed_sem, stats_sem, block_send, block_recv,
 ):
@@ -157,6 +158,16 @@
     above, below, beside = at(z + 1, x), at(z - 1, x), at(z, 1 - x)
     across, twin = (1 - group, seq, tp), (group, seq, 1 - tp)
 
+    loads = [
+        pltpu.make_async_copy(source, target, load_sem.at[index])
+        for index, (source, target) in enumerate((
+            (hidden_hbm, hidden_ref), (gain_hbm, gain_ref), (weight_hbm, weights.at[seq]),
+            (kv_gain_hbm, kv_gain_ref), (owner_hbm, owner_ref), (slot_hbm, slot_ref),
+        ))
+    ]
+    for load in loads:
+        load.start()
+
     barrier = pltpu.get_barrier_semaphore()
     for step in range(1, n_seq):
         pl.semaphore_signal(
@@ -165,18 +176,13 @@
     for peer in (across, twin):
         pl.semaphore_signal(barrier, inc=1, device_id=peer, device_id_type=MESH)
 
-    row_id = lax.broadcasted_iota(jnp.int32, (cols, cols), 0)
-    col_id = lax.broadcasted_iota(jnp.int32, (cols, cols), 1)
-    eye = jnp.where(row_id == col_id, 1.0, 0.0).astype(jnp.bfloat16)
-    weights[seq] = lax.dot_general(
-        eye, weight_ref[...], NT, preferred_element_type=jnp.float32
-    ).astype(jnp.bfloat16)
     pl.semaphore_wait(barrier, n_seq + 1)
 
-    def piece(shard, part, direction, peer):
-        where = weights.at[shard, pl.ds(pl.multiple_of(part * chunk, chunk), chunk), :]
+    def piece(shard, part, direction, peer, source=None):
+        lines = pl.ds(pl.multiple_of(part * chunk, chunk), chunk)
+        where = weights.at[shard, lines, :]
         return pltpu.make_async_remote_copy(
-            src_ref=where,
+            src_ref=where if source is None else source.at[lines, :],
             dst_ref=where,
             send_sem=hop_send.at[shard, part, direction],
             recv_sem=weight_recv.at[shard, part],
@@ -189,16 +195,22 @@
 
     own = seq
     for part in (mine, middle):
-        when_inside(z + 1, lambda: piece(own, part, 0, above).start())
-        when_inside(z - 1, lambda: piece(own, part, 1, below).start())
-        piece(own, part, 2, beside).start()
-
+        when_inside(z + 1, lambda: piece(own, part, 0, above, weight_hbm).start())
+        when_inside(z - 1, lambda: piece(own, part, 1, below, weight_hbm).start())
+        piece(own, part, 2, beside, weight_hbm).start()
+
+    for load in loads:
+        load.wait()
+    for line in range(gain_ref.shape[0]):
+        gain_row[0:1, line * 128 : (line + 1) * 128] = gain_ref[line : line + 1, :].astype(
+            jnp.float32
+        )
     first = pl.multiple_of(tp * rows, rows)
 
     def norm_tile(index, carry):
         tile = hidden_ref[pl.ds(pl.multiple_of(index * 16, 16), 16), :].astype(jnp.float32)
         power = jnp.mean(tile * tile, axis=1, keepdims=True)
-        out = tile * lax.rsqrt(power + EPSILON) * gain_ref[...].astype(jnp.float32)
+        out = tile * lax.rsqrt(power + EPSILON) * gain_row[0:1, :]
         normed[pl.ds(pl.multiple_of(first + index * 16, 16), 16), :] = out.astype(jnp.bfloat16)
         return carry
 
@@ -209,6 +221,32 @@
         device_id=twin, device_id_type=MESH,
     )
     normed_copy.start()
+
+    def arrive(z_from, x_from, part, step=0):
+        def do():
+            shard = z_from * X_COUNT + x_from
+            piece(shard, part, 2, beside).wait_recv()
+            if part is mine:
+                piece(shard, part, 3, across).start()
+            if step == 1:
+                when_inside(z + 1, lambda: piece(shard, part, 0, above).start())
+            if step == -1:
+                when_inside(z - 1, lambda: piece(shard, part, 1, below).start())
+            if step != 0:
+                piece(shard, part, 2, beside).start()
+        when_inside(z_from, do)
+
+    def arrive_column(distance, part):
+        arrive(z - distance, x, part, 1)
+        arrive(z + distance, x, part, -1)
+
+    def arrive_beside(distance, part):
+        arrive(z - distance, 1 - x, part)
+        if distance:
+            arrive(z + distance, 1 - x, part)
+
+    arrive_column(1, mine)
+    arrive_beside(0, mine)
 
     def rank_of(base, block):
         same = [
@@ -224,6 +262,9 @@
         select[pl.ds(block * 64, 64), :] = jnp.where(lane_id - line_id == place, 1.0, 0.0).astype(
             jnp.bfloat16
         )
+
+    arrive_column(2, mine)
+    arrive_beside(1, mine)
 
     slot_total = cache_ref.shape[0] // 64
     lane_in = lax.broadcasted_iota(jnp.int32, (slot_total * 64, 128), 1)
@@ -246,6 +287,9 @@
         placing[:, source * 128 : (source + 1) * 128] = jnp.where(
             line_in == target, 1.0, 0.0
         ).astype(jnp.bfloat16)
+
+    arrive_column(3, mine)
+    arrive_column(1, middle)
 
     rope_half = ROPE // 2
     positions = lax.broadcasted_iota(jnp.int32, (rope_half, tokens), 1) + seq * tokens
@@ -260,44 +304,24 @@
 
     column = lax.broadcasted_iota(jnp.int32, (cols, LAT), 0) + tp * cols
     gain_lane = lax.broadcasted_iota(jnp.int32, (cols, LAT), 1)
-    gain_col = jnp.sum(
-        jnp.where(column == gain_lane, kv_gain_ref[...].astype(jnp.float32), 0.0),
-        axis=1, keepdims=True,
-    )
-
-    def relay(z_from, x_from, onward):
-        def do():
-            shard = z_from * X_COUNT + x_from
-            for part in (mine, middle):
-                piece(shard, part, 2, beside).wait_recv()
-                onward(shard, part)
-                if part is mine:
-                    piece(shard, part, 3, across).start()
-        when_inside(z_from, do)
-
-    def upward(shard, part):
-        when_inside(z + 1, lambda: piece(shard, part, 0, above).start())
-        piece(shard, part, 2, beside).start()
-
-    def downward(shard, part):
-        when_inside(z - 1, lambda: piece(shard, part, 1, below).start())
-        piece(shard, part, 2, beside).start()
-
-    def stop(shard, part):
-        pass
-
-    relay(z, 1 - x, stop)
-    for distance in range(1, Z_COUNT):
-        relay(z - distance, x, upward)
-        relay(z + distance, x, downward)
-        relay(z - distance, 1 - x, stop)
-        relay(z + distance, 1 - x, stop)
+    gain_all = jnp.concatenate(
+        [kv_gain_ref[line : line + 1, :].astype(jnp.float32) for line in range(LAT // 128)], axis=1
+    )
+    gain_col = jnp.sum(jnp.where(column == gain_lane, gain_all, 0.0), axis=1, keepdims=True)
+
+    arrive_beside(2, mine)
+    arrive_column(2, middle)
+    arrive_beside(3, mine)
+    arrive_column(3, middle)
 
     normed_copy.wait()
     total = jnp.zeros((cols, tokens), jnp.float32)
-    for z_at in (z, z + 1 - 2 * (z % 2), (z + 2) % Z_COUNT, Z_COUNT - 1 - z):
-        for x_at in (x, 1 - x):
+    z_order = (z, z + 1 - 2 * (z % 2), (z + 2) % Z_COUNT, Z_COUNT - 1 - z)
+    for x_at in (x, 1 - x):
+        for z_at in z_order:
             shard = z_at * X_COUNT + x_at
+            if x_at is not x:
+                piece(shard, middle, 2, beside).wait_recv()
             if not (z_at is z and x_at is x):
                 piece(shard, other, 3, across).wait_recv()
             features = pl.ds(pl.multiple_of(shard * depth, 128), depth)
@@ -379,9 +403,9 @@
     for step in range(1, n_seq):
         block_copy(seq, (seq + step) % n_seq).wait_send()
     for part in (mine, middle):
-        when_inside(z + 1, lambda: piece(own, part, 0, above).wait_send())
-        when_inside(z - 1, lambda: piece(own, part, 1, below).wait_send())
-        piece(own, part, 2, beside).wait_send()
+        when_inside(z + 1, lambda: piece(own, part, 0, above, weight_hbm).wait_send())
+        when_inside(z - 1, lambda: piece(own, part, 1, below, weight_hbm).wait_send())
+        piece(own, part, 2, beside, weight_hbm).wait_send()
 
     def sent(z_from, x_from, direction, z_to, peer):
         def do():
@@ -409,16 +433,23 @@
     slot_total = 2 * (tokens // 64)
     padded = cols + SCALE_ROWS
     vmem = pl.BlockSpec(memory_space=pltpu.VMEM)
-    smem = pl.BlockSpec(memory_space=pltpu.SMEM)
+    hbm = pl.BlockSpec(memory_space=pltpu.HBM)
     cache, scales = pl.pallas_call(
         fused_kernel,
         out_shape=(
             jax.ShapeDtypeStruct((slot_total * 64, cols), jnp.bfloat16),
             jax.ShapeDtypeStruct((slot_total, 64), jnp.bfloat16),
         ),
-        in_specs=[smem, smem, vmem, vmem, vmem, vmem],
+        in_specs=[hbm] * 6,
         out_specs=(vmem, vmem),
         scratch_shapes=[
+            pltpu.SMEM(block_owner.shape, jnp.int32),
+            pltpu.SMEM(block_slot.shape, jnp.int32),
+            pltpu.VMEM((rows, width), jnp.bfloat16),
+            pltpu.VMEM((width // 128, 128), jnp.bfloat16),
+            pltpu.VMEM((LAT // 128, 128), jnp.bfloat16),
+            pltpu.VMEM((8, width), jnp.float32),
+            pltpu.SemaphoreType.DMA((6,)),
             pltpu.VMEM((n_seq, cols, depth), jnp.bfloat16),
             pltpu.VMEM((tokens, width), jnp.bfloat16),
             pltpu.VMEM((tokens, n_seq * 128), jnp.bfloat16),
@@ -435,11 +466,11 @@
             pltpu.SemaphoreType.DMA((n_seq,)),
         ],
         compiler_params=pltpu.CompilerParams(
-            collective_id=0, has_side_effects=True, vmem_limit_bytes=48 * 1024 * 1024
+            collective_id=0, has_side_effects=True, vmem_limit_bytes=64 * 1024 * 1024 - 65536
         ),
     )(
-        block_owner, block_slot, hidden, in_gain.reshape(1, width), kv_weight,
-        kv_gain.reshape(1, LAT),
+        block_owner, block_slot, hidden, in_gain.reshape(width // 128, 128), kv_weight.T,
+        kv_gain.reshape(LAT // 128, 128),
     )
     return (cache.reshape(slot_total, 64, cols), scales)
 

time: 68.3 us -> 61.2 us (0.90)
  the two profiles are of different devices: /device:TPU:0 before, /device:TPU:11 now
where the time goes in v2:
time: 61.2 us; the launch traced here: 61.1 us
  Pallas kernels  57.4 us (94%)
  local copies, waits for them, and re-layouts  3.01 us (5%)
  between operations  0.64 us (1%)
    pallas_call x1, Pallas kernels, fused(): pl.pallas_call(fused_kernel, out_shape=(jax.ShapeDtypeStruct((slot_total...  57.4 us
    unnamed x2, local copies, waits for them, and re-layouts  3.01 us

profile of v2, /device:TPU:11, one launch (start us, length us, event | category | flops | bytes accessed | tf_op | source)
XLA Modules:
  0.0 61.1 jit_solution(10886972565011264578)
XLA Ops:
  0.6 57.4 %shard_map.77 = (bf16[512,288]{1,0:T(8,128)(2,1)}, bf16[8,64]{1,0:T(8,128)(2,1)}) custom-call(s32[32]{0:T(128)} %owner_hbm.1, s32[32]{0:T(128)} %slot_hbm.1, bf16[128,7168]{1,0:T(8,128)(2,1)} %hidden_hbm.1, bf16[56,128]{1,0:T(8,128)(2,1)} %bitcast.6, bf16[288,896]{1,0:T(8,128)(2,1)} %bitcast.4, bf16[4,128]{1,0:T(4,128)(2,1)} %bitcast.7), custom_call_target="tpu_custom_call" | custom-call | tf_op jit(solution)/shard_map/pallas_call | solution.py:437
  58.0 1.8 %copy.10 = bf16[8,64,288]{2,1,0:T(8,128)(2,1)} copy(bf16[8,64,288]{2,1,0:T(8,128)(2,1)} %bitcast.5) | data formatting | bytes 589824
  59.8 1.2 %copy.11 = bf16[8,64]{1,0:T(8,128)(2,1)} copy(bf16[8,64]{1,0:T(8,128)(2,1)} %get-tuple-element.9) | data formatting | bytes 2048

commit v3 on v2

--- a/solution.py
+++ b/solution.py
@@ -1,3 +1,4 @@
+import functools
 import functools
 import math
 
@@ -140,7 +141,7 @@
     cache_ref, scales_ref,
     owner_ref, slot_ref, hidden_ref, gain_ref, kv_gain_ref, gain_row, load_sem,
     weights, normed, select, placing, outgoing, incoming, stats_out, stats_in,
-    hop_send, weight_recv, normed_sem, stats_sem, block_send, block_recv,
+    gain_col, hop_send, weight_recv, normed_sem, stats_sem, block_send, block_recv,
 ):
     group, seq, tp = lax.axis_index("group"), lax.axis_index("seq"), lax.axis_index("tp")
     n_seq = weights.shape[0]
@@ -221,6 +222,59 @@
         device_id=twin, device_id_type=MESH,
     )
     normed_copy.start()
+
+    def latent_of(part):
+        line = lax.broadcasted_iota(jnp.int32, (chunk, 1), 0) + part * chunk
+        return line + tp * cols < LAT
+
+    def block_copy(source, target, part, lines):
+        place = pl.ds(pl.multiple_of(part * chunk, 16), lines)
+        return pltpu.make_async_remote_copy(
+            src_ref=outgoing.at[target, place, :], dst_ref=incoming.at[source, place, :],
+            send_sem=block_send.at[target, part], recv_sem=block_recv.at[source, part],
+            device_id=(group, target, tp), device_id_type=MESH,
+        )
+
+    def hand_over(values, part, lines):
+        place = pl.ds(pl.multiple_of(part * chunk, 16), lines)
+        for target in range(n_seq):
+            outgoing[target, place, :] = jnp.dot(
+                values, select[:, target * 128 : (target + 1) * 128],
+                preferred_element_type=jnp.float32,
+            ).astype(jnp.bfloat16)
+        for step in range(1, n_seq):
+            block_copy(seq, (seq + step) % n_seq, part, lines).start()
+        incoming[seq, place, :] = outgoing[seq, place, :]
+
+    def project(part, weights_ready):
+        place = pl.ds(pl.multiple_of(part * chunk, chunk), chunk)
+        total = jnp.zeros((chunk, tokens), jnp.float32)
+        for x_at in (x, 1 - x):
+            for z_at in (z, z + 1 - 2 * (z % 2), (z + 2) % Z_COUNT, Z_COUNT - 1 - z):
+                shard = z_at * X_COUNT + x_at
+                weights_ready(shard, z_at, x_at)
+                features = pl.ds(pl.multiple_of(shard * depth, 128), depth)
+                total = total + lax.dot_general(
+                    weights[shard, place, :], normed[:, features], NT,
+                    preferred_element_type=jnp.float32,
+                )
+        latent = latent_of(part)
+        gained = total * gain_col[place, :]
+        power = jnp.sum(jnp.where(latent, total * total, 0.0), axis=0, keepdims=True)
+        latent_peak = jnp.max(jnp.where(latent, jnp.abs(gained), 0.0), axis=0, keepdims=True)
+        lower = total[chunk - ROPE : chunk - rope_half, :]
+        upper = total[chunk - rope_half :, :]
+        turned = jnp.concatenate(
+            [lower * cosine - upper * sine, upper * cosine + lower * sine], axis=0
+        )
+        rope_here = (tp == 1) & (part == 2)
+        rope_peak = jnp.max(jnp.abs(turned), axis=0, keepdims=True)
+        rope_peak = jnp.where(rope_here, rope_peak, 0.0)
+        values = jnp.where(
+            latent, gained, jnp.concatenate([gained[: chunk - ROPE, :], turned], axis=0)
+        )
+        hand_over(values.astype(jnp.bfloat16), part, chunk)
+        return power, latent_peak, rope_peak
 
     def arrive(z_from, x_from, part, step=0):
         def do():
@@ -264,6 +318,7 @@
         )
 
     arrive_column(2, mine)
+    arrive_column(1, middle)
     arrive_beside(1, mine)
 
     slot_total = cache_ref.shape[0] // 64
@@ -289,7 +344,7 @@
         ).astype(jnp.bfloat16)
 
     arrive_column(3, mine)
-    arrive_column(1, middle)
+    arrive_column(2, middle)
 
     rope_half = ROPE // 2
     positions = lax.broadcasted_iota(jnp.int32, (rope_half, tokens), 1) + seq * tokens
@@ -307,39 +362,31 @@
     gain_all = jnp.concatenate(
         [kv_gain_ref[line : line + 1, :].astype(jnp.float32) for line in range(LAT // 128)], axis=1
     )
-    gain_col = jnp.sum(jnp.where(column == gain_lane, gain_all, 0.0), axis=1, keepdims=True)
+    gain_col[...] = jnp.sum(
+        jnp.where(column == gain_lane, gain_all, 0.0), axis=1, keepdims=True
+    )
 
     arrive_beside(2, mine)
-    arrive_column(2, middle)
     arrive_beside(3, mine)
+
+    normed_copy.wait()
+    first_stats = project(mine, lambda shard, z_at, x_at: None)
+
     arrive_column(3, middle)
 
-    normed_copy.wait()
-    total = jnp.zeros((cols, tokens), jnp.float32)
-    z_order = (z, z + 1 - 2 * (z % 2), (z + 2) % Z_COUNT, Z_COUNT - 1 - z)
-    for x_at in (x, 1 - x):
-        for z_at in z_order:
-            shard = z_at * X_COUNT + x_at
-            if x_at is not x:
-                piece(shard, middle, 2, beside).wait_recv()
-            if not (z_at is z and x_at is x):
-                piece(shard, other, 3, across).wait_recv()
-            features = pl.ds(pl.multiple_of(shard * depth, 128), depth)
-            total = total + lax.dot_general(
-                weights[shard], normed[:, features], NT, preferred_element_type=jnp.float32
-            )
-
-    latent = (lax.broadcasted_iota(jnp.int32, (cols, 1), 0) + tp * cols) < LAT
-    gained = total * gain_col
-    power = jnp.sum(jnp.where(latent, total * total, 0.0), axis=0, keepdims=True)
-    latent_peak = jnp.max(jnp.where(latent, jnp.abs(gained), 0.0), axis=0, keepdims=True)
-    lower = total[cols - ROPE : cols - rope_half, :]
-    upper = total[cols - rope_half :, :]
-    turned = jnp.concatenate(
-        [lower * cosine - upper * sine, upper * cosine + lower * sine], axis=0
-    )
-    rope_peak = jnp.max(jnp.abs(turned), axis=0, keepdims=True)
-    rope_peak = jnp.where(tp == 1, rope_peak, 0.0)
+    def by_beside(shard, z_at, x_at):
+        if x_at is not x:
+            piece(shard, middle, 2, beside).wait_recv()
+
+    def by_across(shard, z_at, x_at):
+        if not (z_at is z and x_at is x):
+            piece(shard, other, 3, across).wait_recv()
+
+    stats = [first_stats, project(other, by_across), project(middle, by_beside)]
+    power = sum(one[0] for one in stats)
+    latent_peak = functools.reduce(jnp.maximum, [one[1] for one in stats])
+    rope_peak = functools.reduce(jnp.maximum, [one[2] for one in stats])
+
     stats_out[0:1, :] = power
     stats_out[1:2, :] = latent_peak
     stats_out[2:3, :] = rope_peak
@@ -355,53 +402,52 @@
         jnp.maximum(latent_peak, stats_in[1:2, :]) * inverse,
         jnp.maximum(rope_peak, stats_in[2:3, :]),
     )
-    scale = (peak + EPSILON).astype(jnp.bfloat16)
-    wide_scale = scale.astype(jnp.float32)
-    shaped = jnp.where(
-        latent,
-        gained * inverse,
-        jnp.concatenate([jnp.zeros((cols - ROPE, tokens), jnp.float32), turned], axis=0),
-    )
-    quant = (shaped / wide_scale).astype(jnp.bfloat16)
-    with_scale = jnp.concatenate(
-        [quant, jnp.broadcast_to(wide_scale, (SCALE_ROWS, tokens)).astype(jnp.bfloat16)], axis=0
-    )
-
-    for target in range(n_seq):
-        outgoing[target] = jnp.dot(
-            with_scale, select[:, target * 128 : (target + 1) * 128],
-            preferred_element_type=jnp.float32,
-        ).astype(jnp.bfloat16)
-
-    def block_copy(source, target):
-        return pltpu.make_async_remote_copy(
-            src_ref=outgoing.at[target], dst_ref=incoming.at[source],
-            send_sem=block_send.at[target], recv_sem=block_recv.at[source],
-            device_id=(group, target, tp), device_id_type=MESH,
-        )
-
-    for step in range(1, n_seq):
-        block_copy(seq, (seq + step) % n_seq).start()
-    incoming[seq] = outgoing[seq]
+    scale = (peak + EPSILON).astype(jnp.bfloat16).astype(jnp.float32)
+
+    def terms(value):
+        found = []
+        for _ in range(3):
+            term = value.astype(jnp.bfloat16).astype(jnp.float32)
+            found.append(term)
+            value = value - term
+        return found
+
+    lines = terms(inverse / scale) + terms(1.0 / scale) + [scale]
+    lines = lines + [jnp.zeros((SCALE_ROWS - len(lines), tokens), jnp.float32)]
+    hand_over(jnp.concatenate(lines, axis=0).astype(jnp.bfloat16), 3, SCALE_ROWS)
+
+    column_id = lax.broadcasted_iota(jnp.int32, (cols, 1), 0) + tp * cols
+    slot_id = lax.broadcasted_iota(jnp.int32, (slot_total, 128), 0)
+    lane = lax.broadcasted_iota(jnp.int32, (slot_total, 128), 1)
+    for part in (mine, other, middle):
+        for step in range(1, n_seq):
+            source = (seq + step) % n_seq
+            block_copy(source, source, part, chunk).wait_recv()
     for step in range(1, n_seq):
         source = (seq + step) % n_seq
-        block_copy(source, source).wait_recv()
-    arrived = jnp.concatenate([incoming[source, :cols, :] for source in range(n_seq)], axis=1)
-    cache_ref[...] = lax.dot_general(
-        placing[...], arrived, NT, preferred_element_type=jnp.float32
-    ).astype(jnp.bfloat16)
-    slot_id = lax.broadcasted_iota(jnp.int32, (slot_total, 128), 0)
-    lane = lax.broadcasted_iota(jnp.int32, (slot_total, 128), 1)
+        block_copy(source, source, 3, SCALE_ROWS).wait_recv()
     placed = jnp.zeros((slot_total, 128), jnp.float32)
+    arrived = []
     for source in range(n_seq):
+        factors = incoming[source, cols : cols + SCALE_ROWS, :].astype(jnp.float32)
+        latent_factor = factors[0:1, :] + factors[1:2, :] + factors[2:3, :]
+        rope_factor = factors[3:4, :] + factors[4:5, :] + factors[5:6, :]
+        factor = jnp.where(column_id < LAT, latent_factor, rope_factor)
+        values = incoming[source, :cols, :].astype(jnp.float32)
+        arrived.append((values * factor).astype(jnp.bfloat16))
         low, high = slots[source]
         hit = slot_id == jnp.where(lane < 64, low, high)
-        values = incoming[source, cols : cols + SCALE_ROWS, :].astype(jnp.float32)
-        placed = placed + jnp.where(hit, values[0:slot_total, :], 0.0)
+        placed = placed + jnp.where(hit, factors[6:7, :], 0.0)
+    cache_ref[...] = lax.dot_general(
+        placing[...], jnp.concatenate(arrived, axis=1), NT, preferred_element_type=jnp.float32
+    ).astype(jnp.bfloat16)
     scales_ref[...] = (placed[:, :64] + placed[:, 64:]).astype(jnp.bfloat16)
 
     for step in range(1, n_seq):
-        block_copy(seq, (seq + step) % n_seq).wait_send()
+        target = (seq + step) % n_seq
+        for part in (mine, other, middle):
+            block_copy(seq, target, part, chunk).wait_send()
+        block_copy(seq, target, 3, SCALE_ROWS).wait_send()
     for part in (mine, middle):
         when_inside(z + 1, lambda: piece(own, part, 0, above, weight_hbm).wait_send())
         when_inside(z - 1, lambda: piece(own, part, 1, below, weight_hbm).wait_send())
@@ -458,12 +504,13 @@
             pltpu.VMEM((n_seq, padded, 128), jnp.bfloat16),
             pltpu.VMEM((8, tokens), jnp.float32),
             pltpu.VMEM((8, tokens), jnp.float32),
+            pltpu.VMEM((cols, 1), jnp.float32),
             pltpu.SemaphoreType.DMA((n_seq, 3, 4)),
             pltpu.SemaphoreType.DMA((n_seq, 3)),
             pltpu.SemaphoreType.DMA((2,)),
             pltpu.SemaphoreType.DMA((2,)),
-            pltpu.SemaphoreType.DMA((n_seq,)),
-            pltpu.SemaphoreType.DMA((n_seq,)),
+            pltpu.SemaphoreType.DMA((n_seq, 4)),
+            pltpu.SemaphoreType.DMA((n_seq, 4)),
         ],
         compiler_params=pltpu.CompilerParams(
             collective_id=0, has_side_effects=True, vmem_limit_bytes=64 * 1024 * 1024 - 65536

time: 61.2 us -> 56.3 us (0.920)
  the two profiles are of different devices: /device:TPU:11 before, /device:TPU:0 now
where the time goes in v3:
time: 56.3 us; the launch traced here: 56.1 us
  Pallas kernels  52.4 us (93%)
  local copies, waits for them, and re-layouts  3.01 us (5%)
  between operations  0.64 us (1%)
    pallas_call x1, Pallas kernels, fused(): pl.pallas_call(fused_kernel, out_shape=(jax.ShapeDtypeStruct((slot_total...  52.4 us
    unnamed x2, local copies, waits for them, and re-layouts  3.01 us

profile of v3, /device:TPU:0, one launch (start us, length us, event | category | flops | bytes accessed | tf_op | source)
XLA Modules:
  0.0 56.1 jit_solution(11360301375993539906)
XLA Ops:
  0.6 52.4 %shard_map.77 = (bf16[512,288]{1,0:T(8,128)(2,1)}, bf16[8,64]{1,0:T(8,128)(2,1)}) custom-call(s32[32]{0:T(128)} %owner_hbm.1, s32[32]{0:T(128)} %slot_hbm.1, bf16[128,7168]{1,0:T(8,128)(2,1)} %hidden_hbm.1, bf16[56,128]{1,0:T(8,128)(2,1)} %bitcast.6, bf16[288,896]{1,0:T(8,128)(2,1)} %bitcast.4, bf16[4,128]{1,0:T(4,128)(2,1)} %bitcast.7), custom_call_target="tpu_custom_call" | custom-call | tf_op jit(solution)/shard_map/pallas_call | solution.py:483
  53.1 1.8 %copy.10 = bf16[8,64,288]{2,1,0:T(8,128)(2,1)} copy(bf16[8,64,288]{2,1,0:T(8,128)(2,1)} %bitcast.5) | data formatting | bytes 589824
  54.8 1.2 %copy.11 = bf16[8,64]{1,0:T(8,128)(2,1)} copy(bf16[8,64]{1,0:T(8,128)(2,1)} %get-tuple-element.9) | data formatting | bytes 2048

commit v4 on v3

--- a/solution.py
+++ b/solution.py
@@ -141,7 +141,7 @@
     cache_ref, scales_ref,
     owner_ref, slot_ref, hidden_ref, gain_ref, kv_gain_ref, gain_row, load_sem,
     weights, normed, select, placing, outgoing, incoming, stats_out, stats_in,
-    gain_col, hop_send, weight_recv, normed_sem, stats_sem, block_send, block_recv,
+    gain_col, in_slots, hop_send, weight_recv, normed_sem, stats_sem, block_send, block_recv,
 ):
     group, seq, tp = lax.axis_index("group"), lax.axis_index("seq"), lax.axis_index("tp")
     n_seq = weights.shape[0]
@@ -387,6 +387,16 @@
     latent_peak = functools.reduce(jnp.maximum, [one[1] for one in stats])
     rope_peak = functools.reduce(jnp.maximum, [one[2] for one in stats])
 
+    def place_chunk(part):
+        lines = pl.ds(pl.multiple_of(part * chunk, chunk), chunk)
+        for step in range(1, n_seq):
+            source = (seq + step) % n_seq
+            block_copy(source, source, part, chunk).wait_recv()
+        arrived = jnp.concatenate([incoming[source, lines, :] for source in range(n_seq)], axis=1)
+        in_slots[part] = lax.dot_general(
+            placing[...], arrived, NT, preferred_element_type=jnp.float32
+        )
+
     stats_out[0:1, :] = power
     stats_out[1:2, :] = latent_peak
     stats_out[2:3, :] = rope_peak
@@ -396,6 +406,7 @@
         device_id=twin, device_id_type=MESH,
     )
     stats_copy.start()
+    place_chunk(mine)
     stats_copy.wait()
     inverse = lax.rsqrt((power + stats_in[0:1, :]) / LAT + EPSILON)
     peak = jnp.maximum(
@@ -416,31 +427,30 @@
     lines = lines + [jnp.zeros((SCALE_ROWS - len(lines), tokens), jnp.float32)]
     hand_over(jnp.concatenate(lines, axis=0).astype(jnp.bfloat16), 3, SCALE_ROWS)
 
-    column_id = lax.broadcasted_iota(jnp.int32, (cols, 1), 0) + tp * cols
+    place_chunk(other)
+    place_chunk(middle)
+
     slot_id = lax.broadcasted_iota(jnp.int32, (slot_total, 128), 0)
     lane = lax.broadcasted_iota(jnp.int32, (slot_total, 128), 1)
-    for part in (mine, other, middle):
-        for step in range(1, n_seq):
-            source = (seq + step) % n_seq
-            block_copy(source, source, part, chunk).wait_recv()
     for step in range(1, n_seq):
         source = (seq + step) % n_seq
         block_copy(source, source, 3, SCALE_ROWS).wait_recv()
+    factors = jnp.concatenate(
+        [incoming[source, cols : cols + SCALE_ROWS, :] for source in range(n_seq)], axis=1
+    )
+    by_row = lax.dot_general(placing[...], factors, NT, preferred_element_type=jnp.float32)
+    latent_factor = by_row[:, 0:1] + by_row[:, 1:2] + by_row[:, 2:3]
+    rope_factor = by_row[:, 3:4] + by_row[:, 4:5] + by_row[:, 5:6]
+    column_id = lax.broadcasted_iota(jnp.int32, (1, cols), 1) + tp * cols
+    factor = jnp.where(column_id < LAT, latent_factor, rope_factor)
+    values = jnp.concatenate([in_slots[part] for part in range(3)], axis=1)
+    cache_ref[...] = (values * factor).astype(jnp.bfloat16)
     placed = jnp.zeros((slot_total, 128), jnp.float32)
-    arrived = []
     for source in range(n_seq):
-        factors = incoming[source, cols : cols + SCALE_ROWS, :].astype(jnp.float32)
-        latent_factor = factors[0:1, :] + factors[1:2, :] + factors[2:3, :]
-        rope_factor = factors[3:4, :] + factors[4:5, :] + factors[5:6, :]
-        factor = jnp.where(column_id < LAT, latent_factor, rope_factor)
-        values = incoming[source, :cols, :].astype(jnp.float32)
-        arrived.append((values * factor).astype(jnp.bfloat16))
         low, high = slots[source]
         hit = slot_id == jnp.where(lane < 64, low, high)
-        placed = placed + jnp.where(hit, factors[6:7, :], 0.0)
-    cache_ref[...] = lax.dot_general(
-        placing[...], jnp.concatenate(arrived, axis=1), NT, preferred_element_type=jnp.float32
-    ).astype(jnp.bfloat16)
+        scales_in = incoming[source, cols : cols + SCALE_ROWS, :].astype(jnp.float32)
+        placed = placed + jnp.where(hit, scales_in[6:7, :], 0.0)
     scales_ref[...] = (placed[:, :64] + placed[:, 64:]).astype(jnp.bfloat16)
 
     for step in range(1, n_seq):
@@ -505,6 +515,7 @@
             pltpu.VMEM((8, tokens), jnp.float32),
             pltpu.VMEM((8, tokens), jnp.float32),
             pltpu.VMEM((cols, 1), jnp.float32),
+            pltpu.VMEM((3, slot_total * 64, cols // 3), jnp.float32),
             pltpu.SemaphoreType.DMA((n_seq, 3, 4)),
             pltpu.SemaphoreType.DMA((n_seq, 3)),
             pltpu.SemaphoreType.DMA((2,)),

time: 56.3 us -> 55.7 us (0.989)
  no operation moved by 1% of the time
where the time goes in v4:
time: 55.7 us; the launch traced here: 55.5 us
  Pallas kernels  51.9 us (93%)
  local copies, waits for them, and re-layouts  3.01 us (5%)
  between operations  0.64 us (1%)
    pallas_call x1, Pallas kernels, fused(): pl.pallas_call(fused_kernel, out_shape=(jax.ShapeDtypeStruct((slot_total...  51.9 us
    unnamed x2, local copies, waits for them, and re-layouts  3.01 us

profile of v4, /device:TPU:0, one launch (start us, length us, event | category | flops | bytes accessed | tf_op | source)
XLA Modules:
  0.0 55.5 jit_solution(16985178817620066417)
XLA Ops:
  0.6 51.9 %shard_map.77 = (bf16[512,288]{1,0:T(8,128)(2,1)}, bf16[8,64]{1,0:T(8,128)(2,1)}) custom-call(s32[32]{0:T(128)} %owner_hbm.1, s32[32]{0:T(128)} %slot_hbm.1, bf16[128,7168]{1,0:T(8,128)(2,1)} %hidden_hbm.1, bf16[56,128]{1,0:T(8,128)(2,1)} %bitcast.6, bf16[288,896]{1,0:T(8,128)(2,1)} %bitcast.4, bf16[4,128]{1,0:T(4,128)(2,1)} %bitcast.7), custom_call_target="tpu_custom_call" | custom-call | tf_op jit(solution)/shard_map/pallas_call | solution.py:493
  52.5 1.8 %copy.10 = bf16[8,64,288]{2,1,0:T(8,128)(2,1)} copy(bf16[8,64,288]{2,1,0:T(8,128)(2,1)} %bitcast.5) | data formatting | bytes 589824
  54.3 1.2 %copy.11 = bf16[8,64]{1,0:T(8,128)(2,1)} copy(bf16[8,64]{1,0:T(8,128)(2,1)} %get-tuple-element.9) | data formatting | bytes 2048

commit v5 on v4

--- a/solution.py
+++ b/solution.py
@@ -166,9 +166,6 @@
             (kv_gain_hbm, kv_gain_ref), (owner_hbm, owner_ref), (slot_hbm, slot_ref),
         ))
     ]
-    for load in loads:
-        load.start()
-
     barrier = pltpu.get_barrier_semaphore()
     for step in range(1, n_seq):
         pl.semaphore_signal(
@@ -177,6 +174,8 @@
     for peer in (across, twin):
         pl.semaphore_signal(barrier, inc=1, device_id=peer, device_id_type=MESH)
 
+    for load in loads:
+        load.start()
     pl.semaphore_wait(barrier, n_seq + 1)
 
     def piece(shard, part, direction, peer, source=None):

time: 55.7 us -> 55.7 us (level)
  no operation moved by 1% of the time
where the time goes in v5:
time: 55.7 us; the launch traced here: 55.5 us
  Pallas kernels  51.9 us (93%)
  local copies, waits for them, and re-layouts  3.01 us (5%)
  between operations  0.64 us (1%)
    pallas_call x1, Pallas kernels, fused(): pl.pallas_call(fused_kernel, out_shape=(jax.ShapeDtypeStruct((slot_total...  51.9 us
    unnamed x2, local copies, waits for them, and re-layouts  3.01 us

profile of v5, /device:TPU:0, one launch (start us, length us, event | category | flops | bytes accessed | tf_op | source)
XLA Modules:
  0.0 55.5 jit_solution(9354024749674228569)
XLA Ops:
  0.6 51.9 %shard_map.77 = (bf16[512,288]{1,0:T(8,128)(2,1)}, bf16[8,64]{1,0:T(8,128)(2,1)}) custom-call(s32[32]{0:T(128)} %owner_hbm.1, s32[32]{0:T(128)} %slot_hbm.1, bf16[128,7168]{1,0:T(8,128)(2,1)} %hidden_hbm.1, bf16[56,128]{1,0:T(8,128)(2,1)} %bitcast.6, bf16[288,896]{1,0:T(8,128)(2,1)} %bitcast.4, bf16[4,128]{1,0:T(4,128)(2,1)} %bitcast.7), custom_call_target="tpu_custom_call" | custom-call | tf_op jit(solution)/shard_map/pallas_call | solution.py:492
  52.5 1.8 %copy.10 = bf16[8,64,288]{2,1,0:T(8,128)(2,1)} copy(bf16[8,64,288]{2,1,0:T(8,128)(2,1)} %bitcast.5) | data formatting | bytes 589824
  54.3 1.2 %copy.11 = bf16[8,64]{1,0:T(8,128)(2,1)} copy(bf16[8,64]{1,0:T(8,128)(2,1)} %get-tuple-element.9) | data formatting | bytes 2048
